TPU v7x, 32 devices: a whole 2x2x4 slice. The times are simulated.
32 devices in a mesh: seq: 8 (over z, y), rep: 4 (over x, core).
Axes of the slice: x: 2, y: 2, z: 4, core: 2. Of those that a mesh axis runs over, the one named last changes fastest.
Arguments:
- points: bfloat16 [4096, 512], P(('rep', 'seq')), parts along dimension 0, may hold values from -6 to 6
- decay_one: float32 [8, 4096], P(None, ('rep', 'seq')), parts along dimension 1, may hold values from -1 to 0
- decay_two: float32 [8, 8192], P(None, ('rep', 'seq')), parts along dimension 1, may hold values from -1 to 0
- block_target: int32 [512], P('rep'), parts along dimension 0, may hold values from 0 to 255, as said below
- w_qkv_one: bfloat16 [512, 1536], replicated, may hold values from -0.25 to 0.25
- w_out_one: bfloat16 [512, 512], replicated, may hold values from -0.25 to 0.25
- w_up: bfloat16 [512, 2048], P(None, 'seq'), may hold values from -0.25 to 0.25
- w_down: bfloat16 [2048, 512], P('seq'), may hold values from -0.125 to 0.125
- w_qkv_two: bfloat16 [512, 1536], replicated, may hold values from -0.25 to 0.25
- w_out_two: bfloat16 [512, 512], replicated, may hold values from -0.25 to 0.25
Outputs:
- mixed: bfloat16 [8192, 512], P(('rep', 'seq')), parts along dimension 0
There are 4 independent parts, one for each index of `rep`. A program takes and returns all parts, laid end to end along the dimension named above; an argument that names none is the same for every part. Nothing has to cross between parts.
Inputs may be any that keep to these rules, and one draw needn't show every extreme that they name: `block_target`: entry b is the slot of block b of points; slot g is position g % 32 on device g // 32 of seq, and slots in increasing order give the second sequence. Entries are distinct, every device uses its first slots only, and some device uses all 32. Taken in slot order the blocks go column by column: for one local index j, the j-th block of every device in increasing device order, the columns in some order. At most 4 blocks of one device go to one device, and some device sends that many to one device.
All inputs are finite; a program needn't handle non-finite values.
Results may differ from a plain program's by a relative error of at most 0.018.
Values may be sent and summed in bfloat16 or wider, within the bound.
A program may use at most 128 MiB of HBM per device.

v0:
```python
import jax
import jax.numpy as jnp
from jax import lax
from jax.sharding import PartitionSpec as P

D = 512
MIXER_STREAMS = 8
HEAD_DIM = 64
BR = 8
CAP = 32


epsilon = 1e-05
highest = lax.Precision.HIGHEST


def prefix(value, axis, combine, identity):
    devices, position = (lax.axis_size(axis), lax.axis_index(axis))
    everything = jax.tree.map(
        lambda part, kind: lax.all_gather(part.astype(kind), axis),
        value,
        jax.tree.map(lambda a: jnp.bfloat16 if a.dtype == jnp.float32 else a.dtype, value),
    )
    start = jax.tree.map(
        lambda part, zero: jnp.broadcast_to(jnp.asarray(zero, part.dtype), part.shape),
        value,
        identity,
    )

    def turn(k, before):
        reached = k < position
        new = combine(
            before, jax.tree.map(lambda part, own: part[k].astype(own.dtype), everything, value)
        )
        return jax.tree.map(lambda a, b: jnp.where(reached, a, b), new, before)

    return lax.fori_loop(0, devices, turn, start)


def rms_rows(inputs):
    wide = inputs.astype(jnp.float32)
    return wide * lax.rsqrt(jnp.mean(wide * wide, axis=-1, keepdims=True) + epsilon)


def project(inputs, weight):
    normed = rms_rows(inputs).astype(jnp.bfloat16)
    joined = jnp.dot(normed, weight, preferred_element_type=jnp.float32)
    column = lax.broadcasted_iota(jnp.int32, (1, 3 * D), 1)
    scaled = jnp.where(column < D, joined * HEAD_DIM ** (-0.5), joined)
    return scaled.astype(jnp.bfloat16)


def split_heads(matrix):
    return matrix.reshape(matrix.shape[0], MIXER_STREAMS, HEAD_DIM).transpose(1, 0, 2)


def combine(earlier, later):
    return (earlier[0] + later[0], earlier[1] * jnp.exp(later[0])[:, None, None] + later[1])


def block_summary(key_rows, values, decay):
    cumulative = jnp.cumsum(decay, axis=1)
    decay_total = cumulative[:, -1]
    weighted = key_rows.astype(jnp.float32) * jnp.exp(decay_total[:, None] - cumulative)[:, :, None]
    state_sum = jnp.einsum("hsd,hse->hde", weighted, values.astype(jnp.float32), precision=highest)
    return (cumulative, decay_total, state_sum)


def block_output(queries, key_rows, values, cumulative, entering):
    span = queries.shape[1]
    causal = (
        lax.broadcasted_iota(jnp.int32, (span, span), 0)
        >= lax.broadcasted_iota(jnp.int32, (span, span), 1)
    )[None]
    gap = cumulative[:, :, None] - cumulative[:, None, :]
    weight = jnp.where(causal, jnp.exp(jnp.where(causal, gap, 0.0)), 0.0)
    scores = jnp.einsum("htd,hsd->hts", queries, key_rows, preferred_element_type=jnp.float32)
    weighted = (scores * weight).astype(jnp.bfloat16)
    inner = jnp.einsum("hts,hse->hte", weighted, values, preferred_element_type=jnp.float32)
    carried = jnp.einsum("htd,hde->hte", queries.astype(jnp.float32), entering, precision=highest)
    summed = inner + carried * jnp.exp(cumulative)[:, :, None]
    return summed * lax.rsqrt(jnp.mean(summed * summed, axis=-1, keepdims=True) + epsilon)


def attend_local(joined, decay, chain):
    queries = split_heads(joined[:, :D])
    key_rows = split_heads(joined[:, D : 2 * D])
    values = split_heads(joined[:, 2 * D :])
    total_rows = joined.shape[0]
    device_sum = (
        jnp.zeros((MIXER_STREAMS,), jnp.float32),
        jnp.zeros((MIXER_STREAMS, HEAD_DIM, HEAD_DIM), jnp.float32),
    )
    summary = block_summary(key_rows, values, decay)
    device_sum = combine(device_sum, (summary[1], summary[2]))
    entering = chain(device_sum)[1]
    cumulative, decay_total, state_sum = summary
    result = block_output(queries, key_rows, values, cumulative, entering)
    outputs = result.astype(jnp.bfloat16)
    return outputs.transpose(1, 0, 2).reshape(total_rows, D)


def empty_state():
    return (
        jnp.zeros((MIXER_STREAMS,), jnp.float32),
        jnp.zeros((MIXER_STREAMS, HEAD_DIM, HEAD_DIM), jnp.float32),
    )


def shards(
    points,
    decay_one,
    decay_two,
    block_target,
    w_qkv_one,
    w_out_one,
    w_up,
    w_down,
    w_qkv_two,
    w_out_two,
):

    def chain_first(summary):
        return prefix(summary, "seq", combine, empty_state())

    def chain_second(summary):
        return prefix(summary, "seq", combine, empty_state())

    joined = project(points, w_qkv_one)
    attended = attend_local(joined, decay_one, chain_first)
    first = (
        points.astype(jnp.float32)
        + jnp.dot(attended, w_out_one, preferred_element_type=jnp.float32)
    ).astype(jnp.bfloat16)
    normed = rms_rows(first).astype(jnp.bfloat16)
    hidden = jax.nn.gelu(
        jnp.dot(
            normed,
            lax.all_gather(w_up, "seq", axis=1, tiled=True),
            preferred_element_type=jnp.float32,
        ),
        approximate=True,
    ).astype(jnp.bfloat16)
    down_sum = jnp.dot(
        hidden,
        lax.all_gather(w_down, "seq", axis=0, tiled=True),
        preferred_element_type=jnp.float32,
    )
    layer_out = (first.astype(jnp.float32) + down_sum).astype(jnp.bfloat16)
    seq_count = lax.axis_size("seq")
    position = lax.axis_index("seq")
    local_blocks = layer_out.shape[0] // BR
    per_pair = max(1, CAP // seq_count)
    destination = (block_target // CAP).reshape(seq_count, local_blocks)
    this_block = lax.broadcasted_iota(jnp.int32, (local_blocks, local_blocks), 0)
    other_block = lax.broadcasted_iota(jnp.int32, (local_blocks, local_blocks), 1)
    before = (other_block < this_block)[None]
    same_target = destination[:, :, None] == destination[:, None, :]
    rank_grid = jnp.sum(jnp.where(same_target & before, 1, 0), axis=2).astype(jnp.int32)
    my_target = lax.dynamic_index_in_dim(destination, position, 0, keepdims=False)
    my_rank = lax.dynamic_index_in_dim(rank_grid, position, 0, keepdims=False)
    send_slot = my_target * per_pair + my_rank
    outgoing_ids = lax.broadcasted_iota(jnp.int32, (seq_count * per_pair, local_blocks), 0)
    block_ids = lax.broadcasted_iota(jnp.int32, (seq_count * per_pair, local_blocks), 1)
    pick = outgoing_ids == send_slot[None, :]
    source_block = jnp.sum(jnp.where(pick, block_ids, 0), axis=1)
    occupied = jnp.any(pick, axis=1)
    slot_ids = position * CAP + lax.broadcasted_iota(jnp.int32, (1, CAP), 1)
    match = block_target[:, None] == slot_ids
    all_blocks = lax.broadcasted_iota(jnp.int32, match.shape, 0)
    arriving = jnp.sum(jnp.where(match, all_blocks, 0), axis=0)
    in_use = jnp.any(match, axis=0)
    arrival_slot = arriving // local_blocks * per_pair + rank_grid.reshape(-1)[arriving]
    width = layer_out.shape[1]
    blocks = layer_out.reshape(local_blocks, BR, width)
    chosen = jnp.where(
        occupied[:, None, None], blocks[source_block], jnp.zeros((), layer_out.dtype)
    )
    arrived = lax.all_to_all(
        chosen.reshape(seq_count * per_pair * BR, width),
        "seq",
        split_axis=0,
        concat_axis=0,
        tiled=True,
    )
    width = arrived.shape[1]
    blocks = arrived.reshape(seq_count * per_pair, BR, width)
    chosen = jnp.where(in_use[:, None, None], blocks[arrival_slot], jnp.zeros((), arrived.dtype))
    placed = chosen.reshape(CAP * BR, width)
    joined_two = project(placed, w_qkv_two)
    decay_mask = jnp.repeat(in_use.astype(jnp.float32), BR)
    attended_two = attend_local(joined_two, decay_two * decay_mask[None, :], chain_second)
    return (
        placed.astype(jnp.float32)
        + jnp.dot(attended_two, w_out_two, preferred_element_type=jnp.float32)
    ).astype(jnp.bfloat16)


def solution(mesh):
    in_specs = (
        P(("rep", "seq"), None),
        P(None, ("rep", "seq")),
        P(None, ("rep", "seq")),
        P("rep"),
        P(),
        P(),
        P(None, "seq"),
        P("seq", None),
        P(),
        P(),
    )
    out_specs = P(("rep", "seq"), None)
    return jax.shard_map(shards, mesh=mesh, in_specs=in_specs, out_specs=out_specs, check_vma=False)
```

profile of v0, /device:TPU:0, one launch (start us, length us, event | category | flops | bytes accessed | tf_op | source)
XLA Modules:
  0.0 198.0 jit_solution(17589694517734611159)
XLA Ops:
  6.5 0.7 all-gather.7.cloned.1.call-update
  7.3 0.7 all-gather.9.cloned.1.call-update
  8.0 1.0 reduce_window_sum.40
  9.0 0.2 fusion.69
  9.2 0.2 slice_reduce_fusion.2
  9.5 0.7 and_select_fusion.1
  10.2 0.3 select_reduce_fusion
  10.5 0.6 select_reduce_fusion.1
  11.1 0.6 fusion.68
  11.7 0.8 compare_reduce_fusion
  12.6 1.4 fusion.67
  14.2 0.7 multiply_bitcast_fusion
  14.9 0.6 reduce-window.6
  15.5 0.2 slice_reduce_fusion
  15.8 0.2 fusion.70
  16.0 0.2 slice_reduce_fusion.1
  16.2 1.2 dynamic-slice
  18.0 0.2 dynamic-update-slice.1
  18.2 0.2 dynamic-update-slice
  18.5 23.3 %all-reduce.2 = (bf16[64]{0:T(256)(128)(2,1)S(1)}, bf16[64]{0:T(256)(128)(2,1)S(1)}) all-reduce(bf16[64]{0:T(256)(128)(2,1)S(1)} %dynamic-update-slice, bf16[64]{0:T(256)(128)(2,1)S(1)} %dynamic-update-slice.1), channel_id=2, replica_groups=mesh['seq'=8,'rep'=4] {'seq'}, use_global_device_ids=true, to_apply=%add | all-reduce | flops 128 | bytes 512
  41.8 1.0 fusion.41
  42.8 1.9 fusion.25
  44.8 0.1 copy.49
  44.9 0.1 copy.50
  45.1 0.3 fusion.7
  45.4 34.9 %all-gather.1 = bf16[64,64,64]{2,1,0:T(8,128)(2,1)S(1)} all-gather(bf16[8,64,64]{2,1,0:T(8,128)(2,1)S(1)} %fusion.7), channel_id=3, replica_groups=mesh['seq'=8,'rep'=4] {'seq'}, dimensions={0}, use_global_device_ids=true | all-gather | bytes 589824 | tf_op jit(solution)/shard_map/all_gather | solution.py:20
  80.3 0.1 copy.48
  80.4 0.6 fusion.72
  81.0 0.7 broadcast_in_dim.141
  81.9 0.6 fusion.71
  82.6 0.7 gather_fusion.1
  83.3 1.2 while.28
  84.5 0.4 fusion.84
  84.9 0.5 multiply_reduce_fusion.3
  85.6 0.3 multiply_reduce_fusion.2
  86.0 43.3 %all-gather.9.cloned.1.call-done = bf16[2048,512]{1,0:T(8,128)(2,1)} async-done(((bf16[256,512]{1,0:T(8,128)(2,1)}), bf16[2048,512]{1,0:T(8,128)(2,1)}) %all-gather.9.cloned.1.call-update) | async-done | bytes 2097168 | tf_op jit(solution)/shard_map/all_gather | solution.py:146
  129.3 3.2 %fusion.12 = bf16[16,8,512]{2,1,0:T(8,128)(2,1)S(1)} fusion(f32[128,512]{1,0:T(8,128)S(1)} %get-tuple-element.269, bf16[2048,512]{1,0:T(8,128)(2,1)} %all-gather.9.cloned.1.call-done, bf16[512,2048]{1,0:T(8,128)(2,1)} %all-gather.7.cloned.1.call-done, f32[128]{0:T(128)S(1)} %add_rsqrt_fusion.1), kind=kOutput, calls=%fused_computation.29 | convolution fusion | flops 539492352 | bytes 4588032 | tf_op jit(solution)/shard_map/dot_general | solution.py:144
  132.5 0.6 gather_fusion
  133.0 0.8 bitcast_select_fusion.1
  133.8 3.4 %all-to-all-start = ((bf16[8,32,512]{2,1,0:T(8,128)(2,1)}), bf16[8,32,512]{2,1,0:T(8,128)(2,1)S(1)}, u32[]{:S(2)}, u32[]{:S(2)}) async-start(bf16[8,32,512]{2,1,0:T(8,128)(2,1)} %bitcast_select_fusion.1), calls=%async_computation | async-start | bytes 524288 | tf_op jit(solution)/shard_map/all_to_all | solution.py:179
  137.6 8.1 %all-to-all-done = bf16[8,32,512]{2,1,0:T(8,128)(2,1)S(1)} async-done(((bf16[8,32,512]{2,1,0:T(8,128)(2,1)}), bf16[8,32,512]{2,1,0:T(8,128)(2,1)S(1)}, u32[]{:S(2)}, u32[]{:S(2)}) %all-to-all-start) | async-done | bytes 262176 | tf_op jit(solution)/shard_map/all_to_all | solution.py:179
  145.8 0.6 gather_fusion.2
  146.4 0.2 multiply_reduce_fusion.1
  146.7 0.6 fusion.2
  147.3 0.8 fusion.81
  148.1 0.1 copy.53
  148.2 0.1 copy.54
  148.4 0.7 copy-done.1
  149.1 0.4 fusion.11
  149.5 33.1 %all-gather.3 = bf16[64,64,64]{2,1,0:T(8,128)(2,1)S(1)} all-gather(bf16[8,64,64]{2,1,0:T(8,128)(2,1)S(1)} %fusion.11), channel_id=5, replica_groups=mesh['seq'=8,'rep'=4] {'seq'}, dimensions={0}, use_global_device_ids=true | all-gather | bytes 589824 | tf_op jit(solution)/shard_map/all_gather | solution.py:20
  182.6 1.2 while.29
  182.6 0.1 fusion.109
  182.7 0.1 fusion.109
  182.9 0.1 fusion.109
  183.0 0.1 fusion.109
  183.2 0.1 fusion.109
  183.3 0.1 fusion.109
  183.5 0.1 fusion.109
  183.6 0.1 fusion.109
  183.8 1.1 copy.52
  184.8 0.4 fusion.85
  185.3 2.7 %multiply_reduce_fusion = (f32[8,256]{1,0:T(8,128)S(1)}, f32[8,256,64]{1,2,0:T(8,128)}) fusion(f32[8,256,64]{1,2,0:T(8,128)S(1)} %fusion.85, f32[8,256]{1,0:T(8,128)S(1)} %get-tuple-element.261, bf16[8,256,64]{1,2,0:T(8,128)(2,1)} %bitcast.139, bf16[8,256,64]{1,2,0:T(8,128)(2,1)S(1)} %bitcast.141, bf16[8,256,64]{1,2,0:T(8,128)(2,1)S(1)} %bitcast.137, ...), kind=kOutput, calls=%fused_computation.49 | convolution fusion | flops 137361408 | bytes 1925120 | tf_op jit(solution)/shard_map/hts,hse->hte/dot_general | solution.py:79
  188.0 1.1 fusion.30
  189.1 2.1 %fusion.4 = bf16[256,512]{1,0:T(8,128)(2,1)} fusion(bf16[256,512]{0,1:T(8,128)(2,1)S(1)} %bitcast.149, bf16[512,512]{1,0:T(8,128)(2,1)} %param.23, bf16[32,8,512]{2,1,0:T(8,128)(2,1)S(1)} %gather_fusion.2, pred[256]{0:T(512)(128)(4,1)S(1)} %broadcast_in_dim.137), kind=kOutput, calls=%fused_computation.16 | convolution fusion | flops 134742016 | bytes 1310976 | tf_op jit(solution)/shard_map/dot_general | solution.py:195
  (76 shorter events, 2.6 us)
Async XLA Ops:
  6.5 140.1 %copy-start = (bf16[512,1536]{1,0:T(8,128)(2,1)S(1)}, bf16[512,1536]{1,0:T(8,128)(2,1)}, u32[]{:S(2)}) copy-start(bf16[512,1536]{1,0:T(8,128)(2,1)} %param.22) | copy-start | bytes 4718596
  6.5 79.4 %all-gather.7.cloned.1.call-start = ((), (), s32[]{:S(2)}) async-start(), calls=%async_computation.1 | async-start | bytes 2359296 | tf_op jit(solution)/shard_map/all_gather | solution.py:139
  7.3 122.0 %all-gather.9.cloned.1.call-start = ((), (), s32[]{:S(2)}) async-start(), calls=%async_computation.2 | async-start | bytes 2359296 | tf_op jit(solution)/shard_map/all_gather | solution.py:146
  84.5 1.0 copy-start.2
  84.5 1.1 copy-start.3
  84.5 1.4 copy-start.4
  133.8 11.9 %all-to-all-start = ((bf16[8,32,512]{2,1,0:T(8,128)(2,1)}), bf16[8,32,512]{2,1,0:T(8,128)(2,1)S(1)}, u32[]{:S(2)}, u32[]{:S(2)}) async-start(bf16[8,32,512]{2,1,0:T(8,128)(2,1)} %bitcast_select_fusion.1), calls=%async_computation | async-start | bytes 524288 | tf_op jit(solution)/shard_map/all_to_all | solution.py:179
  148.4 0.7 copy-start.1
Sparse Core Ops, SparseCore 0:
  9.4 70.4 all-gather.6
  82.0 47.1 all-gather.8
where the time goes:
time: 199 us; the launch traced here: 198 us
  blocking collectives  91.3 us (46%)
  waiting for transfers between devices  52.9 us (27%)
  between operations  14.3 us (7%)
  other arithmetic  13.4 us (7%)
  matrix products  12.9 us (6%)
  local copies, waits for them, and re-layouts  9.39 us (5%)
  starting transfers between devices  3.45 us (2%)
    all_gather x2, blocking collectives, prefix(): lax.all_gather(part.astype(kind), axis)  68 us
    all_gather x1, waiting for transfers between devices, shards(): lax.all_gather(w_down, 'seq', axis=0, tiled=True)  43.3 us
    unnamed x1, blocking collectives  23.3 us
    all_to_all x1, waiting for transfers between devices, shards(): lax.all_to_all(chosen.reshape(seq_count * per_pair * BR, width), 'seq', s...  8.15 us
  transfers between devices with their start and end apart: 3, of which 2 were waited for; matrix products, arithmetic and copies ran while one was open for 10% of the time, Pallas kernels for 0%

commit v1 on v0

v1 whole, which is shorter than its diff:
```python
import functools

import jax
import jax.numpy as jnp
from jax import lax
from jax.experimental import pallas as pl
from jax.experimental.pallas import tpu as pltpu
from jax.sharding import PartitionSpec as P

MIXER_STREAMS = 8
HEAD_DIM = 64
BR = 8
CAP = 32
LANES = 128
EPS = 1e-05
F32 = jnp.float32
BF16 = jnp.bfloat16
MESH = pl.DeviceIdType.MESH
UNROLL = 16


def dot(a, b):
    return jnp.dot(a, b, preferred_element_type=F32)


def dot_nt(a, b):
    return lax.dot_general(a, b, (((1,), (1,)), ((), ())), preferred_element_type=F32)


def dot_tn(a, b):
    return lax.dot_general(a, b, (((0,), (0,)), ((), ())), preferred_element_type=F32)


def iota(shape, dim):
    return lax.broadcasted_iota(jnp.int32, shape, dim)


def ones_where(mask):
    return jnp.where(mask, 1.0, 0.0).astype(BF16)


def split3(x):
    hi = x.astype(BF16)
    rest = x - hi.astype(F32)
    mid = rest.astype(BF16)
    low = (rest - mid.astype(F32)).astype(BF16)
    return hi, mid, low


def rms(x):
    return x * lax.rsqrt(jnp.mean(x * x, axis=-1, keepdims=True) + EPS)


def gelu(x):
    return 0.5 * x * (1.0 + jnp.tanh(0.7978845608028654 * (x + 0.044715 * (x * x * x))))


def loop(start, stop, body):
    if stop - start <= UNROLL:
        for i in range(start, stop):
            body(i)
    else:
        def step(i, carry):
            body(i)
            return carry

        lax.fori_loop(start, stop, step, 0)


def log2(n):
    assert n & (n - 1) == 0
    return n.bit_length() - 1


def project(x, weight, joined):
    width = x.shape[1]
    normed = rms(x).astype(BF16)
    joined[:, :width] = (dot(normed, weight[:, :width]) * HEAD_DIM**-0.5).astype(BF16)
    joined[:, width:] = dot(normed, weight[:, width:]).astype(BF16)


def kernel(
    seq, reps, owners,
    points, decay_one, decay_two, target, w_qkv_one, w_out_one, w_up, w_down, w_qkv_two, w_out_two,
    out,
    wq1, wo1, wq2, wo2, up, down,
    joined_one, joined_two, num_one, num_two, att_one, att_two,
    a_send, a_recv, b_send, b_recv, blk_send, blk_recv, acc,
    load_sem, own_sem, ring_send, ring_recv, core_send, core_recv,
    ex_send, ex_recv,
):
    me = lax.axis_index("seq")
    rep = lax.axis_index("rep")
    rows, width = points.shape
    rows_two = out.shape[0]
    half = seq // 2
    halves = 2 if reps % 2 == 0 else 1
    part = width // halves
    mine = rep % halves
    partner = rep + 1 - 2 * (rep % 2)
    groups = width // LANES
    per_group = owners // groups
    state_rows = HEAD_DIM // per_group
    pair_rows = blk_send.shape[1]

    loads = [
        pltpu.make_async_copy(src, dst, load_sem.at[i])
        for i, (src, dst) in enumerate(
            ((w_qkv_one, wq1), (w_out_one, wo1), (w_qkv_two, wq2), (w_out_two, wo2))
        )
    ]
    loads[0].start()
    own = [
        pltpu.make_async_copy(w_up, up.at[me], own_sem.at[0]),
        pltpu.make_async_copy(w_down, down.at[me], own_sem.at[1]),
    ]

    barrier = pltpu.get_barrier_semaphore()

    def greet(i):
        pl.semaphore_signal(
            barrier, inc=1, device_id={"seq": lax.rem(me + i, seq)}, device_id_type=MESH
        )

    loop(1, seq, greet)
    if halves == 2:
        pl.semaphore_signal(barrier, inc=1, device_id={"rep": partner}, device_id_type=MESH)
    pl.semaphore_wait(barrier, seq - 1 + (1 if halves == 2 else 0))

    place = jnp.where(me % 2 == 0, me // 2, seq - 1 - me // 2)

    def at_place(p):
        q = lax.rem(p + 2 * seq, seq)
        return jnp.where(q < half, 2 * q, 2 * (seq - 1 - q) + 1)

    neighbour = (at_place(place + 1), at_place(place - 1))

    def piece(w, s):
        if w == 0:
            return up.at[s, pl.ds(pl.multiple_of(mine * part, part), part), :]
        return down.at[s, :, pl.ds(pl.multiple_of(mine * part, part), part)]

    def own_piece(w):
        if w == 0:
            return w_up.at[pl.ds(pl.multiple_of(mine * part, part), part), :]
        return w_down.at[:, pl.ds(pl.multiple_of(mine * part, part), part)]

    def origin(way, k):
        return at_place(place - k if way == 0 else place + k)

    def ring(way, w, k, first=False):
        where = piece(w, me if first else origin(way, k - 1))
        return pltpu.make_async_remote_copy(
            src_ref=own_piece(w) if first else where,
            dst_ref=where,
            send_sem=ring_send.at[way, w, k - 1],
            recv_sem=ring_recv.at[way, w, k - 1],
            device_id={"seq": neighbour[way]},
            device_id_type=MESH,
        )

    def ring_arrival(way, w, k):
        where = piece(w, origin(way, k))
        return pltpu.make_async_remote_copy(
            src_ref=where,
            dst_ref=where,
            send_sem=ring_send.at[way, w, k - 1],
            recv_sem=ring_recv.at[way, w, k - 1],
            device_id={"seq": neighbour[way]},
            device_id_type=MESH,
        )

    def core(way, w, k):
        where = piece(w, origin(way, k))
        return pltpu.make_async_remote_copy(
            src_ref=where,
            dst_ref=where,
            send_sem=core_send.at[way, w, k - 1],
            recv_sem=core_recv.at[way, w, k - 1],
            device_id={"rep": partner},
            device_id_type=MESH,
        )

    both = [(way, w) for w in range(2) for way in range(2)]
    last = [(0, 0), (1, 1)]

    def routes(k):
        return last if isinstance(k, int) and k == half else both

    def relay(k, routes_now, routes_next):
        for way, w in routes_now:
            ring_arrival(way, w, k).wait_recv()
            if (way, w) in routes_next:
                ring(way, w, k + 1).start()
            if halves == 2:
                core(way, w, k).start()

    def relay_step(k):
        relay(k, routes(k), routes(k + 1) if k < half else [])

    for way, w in routes(1):
        ring(way, w, 1, first=True).start()
    for copy in loads[1:] + own:
        copy.start()

    def exchange(index, source, target_buf, count):
        def copy(i, peer):
            return pltpu.make_async_remote_copy(
                src_ref=source.at[peer],
                dst_ref=target_buf.at[me],
                send_sem=ex_send.at[index, i],
                recv_sem=ex_recv.at[index, i],
                device_id={"seq": peer},
                device_id_type=MESH,
            )

        def arrival(i):
            src = lax.rem(me - i + seq, seq)
            return pltpu.make_async_remote_copy(
                src_ref=target_buf.at[src],
                dst_ref=target_buf.at[src],
                send_sem=ex_send.at[index, i],
                recv_sem=ex_recv.at[index, i],
                device_id={"seq": lax.rem(me + i, seq)},
                device_id_type=MESH,
            )

        return copy, arrival

    def maybe(cond, all_true, body):
        if all_true:
            body()
        else:
            pl.when(cond)(body)

    def to_owners(index, layer):
        copy, arrival = exchange(index, a_send.at[layer], a_recv.at[layer], owners)

        def start(i):
            peer = lax.rem(me + i, seq)
            maybe(peer < owners, owners == seq, lambda: copy(i, peer).start())

        def finish(i):
            peer = lax.rem(me + i, seq)
            maybe(me < owners, owners == seq, lambda: arrival(i).wait_recv())

        def sent(i):
            peer = lax.rem(me + i, seq)
            maybe(peer < owners, owners == seq, lambda: copy(i, peer).wait_send())

        return start, finish, sent

    def from_owners(index, layer):
        copy, arrival = exchange(index, b_send.at[layer], b_recv.at[layer], seq)

        def start(i):
            peer = lax.rem(me + i, seq)
            maybe(me < owners, owners == seq, lambda: copy(i, peer).start())

        def finish(i):
            src = lax.rem(me - i + seq, seq)
            maybe(src < owners, owners == seq, lambda: arrival(i).wait_recv())

        def sent(i):
            peer = lax.rem(me + i, seq)
            maybe(me < owners, owners == seq, lambda: copy(i, peer).wait_send())

        return start, finish, sent

    def sums(decay):
        span = decay.shape[1]
        later = ones_where(iota((span, span), 0) >= iota((span, span), 1))
        earlier = ones_where(iota((span, span), 0) <= iota((span, span), 1))
        heads = ones_where(iota((width, MIXER_STREAMS), 0) // HEAD_DIM == iota((width, MIXER_STREAMS), 1))
        wide = jnp.zeros((span, width), F32)
        flat = jnp.zeros((MIXER_STREAMS, span), F32)
        for piece_of in split3(decay):
            wide = wide + dot_nt(later, dot(heads, piece_of).astype(BF16))
            flat = flat + dot(piece_of, earlier)
        return wide, flat

    def summarise(joined, wide, layer):
        span = joined.shape[0]
        total = wide[span - 1 : span, :]
        keys = (joined[:, width : 2 * width].astype(F32) * jnp.exp(total - wide)).astype(BF16)
        values = joined[:, 2 * width :]
        first_head = iota((HEAD_DIM, LANES), 1) < HEAD_DIM
        tail_row = iota((16, LANES), 0)
        for g in range(groups):
            cols = slice(g * LANES, (g + 1) * LANES)
            state = dot_tn(keys[:, cols], values[:, cols])
            packed = jnp.where(first_head, state[:HEAD_DIM], state[HEAD_DIM:]).astype(BF16)
            hi, mid, low = (jnp.broadcast_to(t.astype(F32), (16, LANES)) for t in split3(total[:, cols]))
            tail = jnp.where(tail_row == 0, hi, jnp.where(tail_row == 1, mid, jnp.where(tail_row == 2, low, 0.0)))
            tail = tail.astype(BF16)
            for r in range(per_group):
                o = g * per_group + r
                a_send[layer, o, :state_rows] = packed[r * state_rows : (r + 1) * state_rows]
                a_send[layer, o, state_rows:] = tail

    def own_summary(layer):
        maybe(me < owners, owners == seq, lambda: store(a_recv, layer, me, a_send[layer, me]))

    def store(ref, layer, index, value):
        ref[layer, index] = value

    def prefix(layer):
        def step(j, before):
            b_send[layer, j] = before.astype(BF16)
            message = a_recv[layer, j].astype(F32)
            total = message[state_rows : state_rows + 1] + message[state_rows + 1 : state_rows + 2]
            total = total + message[state_rows + 2 : state_rows + 3]
            return before * jnp.exp(total) + message[:state_rows]

        def run():
            before = jnp.zeros((state_rows, LANES), F32)
            if seq <= UNROLL:
                for j in range(seq):
                    before = step(j, before)
            else:
                lax.fori_loop(0, seq, step, before)
            b_recv[layer, me] = b_send[layer, me]

        maybe(me < owners, owners == seq, run)

    def inner(joined, wide, flat, num, g):
        span = joined.shape[0]
        cols = slice(g * LANES, (g + 1) * LANES)
        query = joined[:, cols]
        key = joined[:, width + g * LANES : width + (g + 1) * LANES]
        value = joined[:, 2 * width + g * LANES : 2 * width + (g + 1) * LANES]
        causal = iota((span, span), 0) >= iota((span, span), 1)
        total = jnp.zeros((span, LANES), F32)
        for a in range(2):
            mask = ones_where(iota((1, LANES), 1) // HEAD_DIM == a)
            h = 2 * g + a
            gap = wide[:, h * HEAD_DIM : h * HEAD_DIM + 1] - flat[h : h + 1, :]
            weight = jnp.exp(jnp.where(causal, gap, -1e30))
            scores = dot_nt(query, key * mask)
            total = total + dot((scores * weight).astype(BF16), value * mask)
        num[:, cols] = total

    def finish_heads(joined, wide, num, att, layer):
        same = ones_where(iota((LANES, LANES), 0) // HEAD_DIM == iota((LANES, LANES), 1) // HEAD_DIM)
        for g in range(groups):
            cols = slice(g * LANES, (g + 1) * LANES)
            packed = jnp.concatenate(
                [b_recv[layer, g * per_group + r] for r in range(per_group)], axis=0
            )
            entering = jnp.concatenate([packed, packed], axis=0) * same
            total = num[:, cols] + dot(joined[:, cols], entering) * jnp.exp(wide[:, cols])
            mean = dot((total * total).astype(BF16), same) * (1.0 / HEAD_DIM)
            att[:, cols] = (total * lax.rsqrt(mean + EPS)).astype(BF16)

    x = points[...].astype(F32)
    loads[0].wait()
    project(x, wq1, joined_one)
    wide, flat = sums(decay_one[...])
    summarise(joined_one, wide, 0)
    start, finish, sent_a1 = to_owners(0, 0)
    loop(1, seq, start)
    own_summary(0)
    many = half > UNROLL // 2
    pumps = iter(()) if many else iter(range(1, half + 1))

    def pump():
        k = next(pumps, None)
        if k is not None:
            relay_step(k)

    pump()
    for g in range(groups):
        inner(joined_one, wide, flat, num_one, g)
    loop(1, seq, finish)
    prefix(0)
    start, finish, sent_b1 = from_owners(1, 0)
    loop(1, seq, start)
    pump()

    blocks = target.shape[1]
    shift_cap, shift_row = log2(CAP), log2(BR)
    local_blocks = rows // BR
    shift_local = log2(local_blocks)
    slot = target[...]
    device_of = jnp.broadcast_to(lax.shift_right_logical(slot, shift_cap).astype(F32), (8, blocks)).astype(BF16)
    slot_in = lax.bitwise_and(slot, CAP - 1)
    token_block = iota((rows, blocks), 0) // BR + me * local_blocks
    pick = ones_where(token_block == iota((rows, blocks), 1))
    to_row = dot_nt(device_of, pick)[0:1]
    to_col = dot_nt(pick, device_of)[:, 0:1]
    t0, t1 = iota((rows, rows), 0), iota((rows, rows), 1)
    before = (t0 // BR < t1 // BR) & (t0 % BR == 0) & (to_row == to_col)
    rank = jnp.sum(jnp.where(before, 1.0, 0.0), axis=0, keepdims=True)
    send_row = to_row * pair_rows + rank * BR + (iota((1, rows), 1) % BR).astype(F32)
    all_rows = seq * pair_rows
    scatter = ones_where(iota((all_rows, rows), 0).astype(F32) == send_row)

    here = lax.shift_right_logical(slot, shift_cap) == me
    here_rows = ones_where(jnp.broadcast_to(here, (8, blocks)))
    chunk = min(LANES, blocks)
    c0, c1 = iota((chunk, chunk), 0), iota((chunk, chunk), 1)
    lower = ones_where((c0 // local_blocks == c1 // local_blocks) & (c1 < c0))
    same_index = ones_where(c0 == c1)
    placing = jnp.zeros((rows_two, all_rows), F32)
    used = jnp.zeros((8, rows_two), F32)
    row_slot = iota((rows_two, chunk), 0) // BR
    in_row = iota((chunk, all_rows), 1) // BR * BR
    for c in range(blocks // chunk):
        cols = slice(c * chunk, (c + 1) * chunk)
        rank_col = dot_nt(lower, here_rows[:, cols])[:, 0:1]
        here_col = dot_nt(same_index, here_rows[:, cols])[:, 0:1]
        block_col = (iota((chunk, 1), 0) + c * chunk) // local_blocks
        base = block_col.astype(F32) * pair_rows + rank_col * BR
        base = jnp.where(here_col > 0.5, base, -1.0)
        taken = ones_where((row_slot == slot_in[:, cols]) & here[:, cols])
        placing = placing + dot(taken, ones_where(base == in_row.astype(F32)))
        used = used + dot_nt(jnp.ones((8, chunk), BF16), taken)
    sub = iota((rows_two, all_rows), 0) % BR == iota((rows_two, all_rows), 1) % BR
    gather = jnp.where(sub, placing, 0.0).astype(BF16)
    wide_two, flat_two = sums(decay_two[...] * used[0:1])

    loop(1, seq, finish)
    finish_heads(joined_one, wide, num_one, att_one, 0)
    loads[1].wait()
    first = (x + dot(att_one[...], wo1[...])).astype(BF16)
    normed = rms(first.astype(F32)).astype(BF16)

    def feed(s):
        hidden = gelu(dot(normed, up[s])).astype(BF16)
        acc[...] += dot(hidden, down[s])

    acc[...] = first.astype(F32)
    pump()
    for copy in own:
        copy.wait()
    feed(me)

    def take(k):
        if halves == 2:
            for way, w in routes(k):
                core(way, w, k).wait_recv()
        feed(origin(0, k))
        if not (isinstance(k, int) and k == half):
            feed(origin(1, k))

    if many:
        loop(1, half - 1, lambda k: relay(k, both, both))
        relay(half - 1, both, last)
        relay(half, last, [])
        loop(1, half, take)
        take(half)
    else:
        for k in range(1, half + 1):
            take(k)
            pump()

    layer_out = acc[...].astype(BF16)
    chosen = dot(scatter, layer_out).astype(BF16)
    for j in range(seq):
        blk_send[j] = chosen[j * pair_rows : (j + 1) * pair_rows]
    move, moved = exchange(2, blk_send, blk_recv, seq)
    loop(1, seq, lambda i: move(i, lax.rem(me + i, seq)).start())
    blk_recv[me] = blk_send[me]
    loads[2].wait()
    loop(1, seq, lambda i: moved(i).wait_recv())
    placed = dot(gather, blk_recv[...].reshape(all_rows, width))

    project(placed, wq2, joined_two)
    summarise(joined_two, wide_two, 1)
    start, finish, sent_a2 = to_owners(3, 1)
    loop(1, seq, start)
    own_summary(1)
    for g in range(groups // 2):
        inner(joined_two, wide_two, flat_two, num_two, g)
    loop(1, seq, finish)
    prefix(1)
    start, finish, sent_b2 = from_owners(4, 1)
    loop(1, seq, start)
    for g in range(groups // 2, groups):
        inner(joined_two, wide_two, flat_two, num_two, g)
    loads[3].wait()
    loop(1, seq, finish)
    finish_heads(joined_two, wide_two, num_two, att_two, 1)
    out[...] = (placed + dot(att_two[...], wo2[...])).astype(BF16)

    for sent in (sent_a1, sent_b1, sent_a2, sent_b2):
        loop(1, seq, sent)
    loop(1, seq, lambda i: move(i, lax.rem(me + i, seq)).wait_send())
    for way, w in routes(1):
        ring(way, w, 1, first=True).wait_send()

    def relayed(k):
        for way, w in routes(k):
            if not (isinstance(k, int) and k == 1):
                ring(way, w, k).wait_send()
            if halves == 2:
                core(way, w, k).wait_send()

    relayed(1)
    loop(2, half, relayed)
    relayed(half)


def shards(seq, reps, points, decay_one, decay_two, block_target, w_qkv_one, w_out_one, w_up, w_down, w_qkv_two, w_out_two):
    rows, width = points.shape
    rows_two = CAP * BR
    groups = width // LANES
    owners = min(seq, 4 * groups)
    state_rows = HEAD_DIM * groups // owners
    pair_rows = max(16, max(1, CAP // seq) * BR)
    half = seq // 2
    hidden = w_up.shape[1]
    vmem = pl.BlockSpec(memory_space=pltpu.VMEM)
    anywhere = pl.BlockSpec(memory_space=pl.ANY)
    dma = pltpu.SemaphoreType.DMA
    return pl.pallas_call(
        functools.partial(kernel, seq, reps, owners),
        out_shape=jax.ShapeDtypeStruct((rows_two, width), BF16),
        in_specs=[vmem] * 4 + [anywhere] * 6,
        out_specs=vmem,
        scratch_shapes=[
            pltpu.VMEM(w_qkv_one.shape, BF16),
            pltpu.VMEM(w_out_one.shape, BF16),
            pltpu.VMEM(w_qkv_two.shape, BF16),
            pltpu.VMEM(w_out_two.shape, BF16),
            pltpu.VMEM((seq, width, hidden), BF16),
            pltpu.VMEM((seq, hidden, width), BF16),
            pltpu.VMEM((rows, 3 * width), BF16),
            pltpu.VMEM((rows_two, 3 * width), BF16),
            pltpu.VMEM((rows, width), F32),
            pltpu.VMEM((rows_two, width), F32),
            pltpu.VMEM((rows, width), BF16),
            pltpu.VMEM((rows_two, width), BF16),
            pltpu.VMEM((2, owners, state_rows + 16, LANES), BF16),
            pltpu.VMEM((2, seq, state_rows + 16, LANES), BF16),
            pltpu.VMEM((2, seq, state_rows, LANES), BF16),
            pltpu.VMEM((2, owners, state_rows, LANES), BF16),
            pltpu.VMEM((seq, pair_rows, width), BF16),
            pltpu.VMEM((seq, pair_rows, width), BF16),
            pltpu.VMEM((rows, width), F32),
            dma((4,)),
            dma((2,)),
            dma((2, 2, half)),
            dma((2, 2, half)),
            dma((2, 2, half)),
            dma((2, 2, half)),
            dma((5, seq)),
            dma((5, seq)),
        ],
        compiler_params=pltpu.CompilerParams(
            collective_id=0, has_side_effects=True, vmem_limit_bytes=56 * 1024 * 1024
        ),
    )(
        points, decay_one, decay_two, block_target.reshape(1, -1),
        w_qkv_one, w_out_one, w_up, w_down, w_qkv_two, w_out_two,
    )


def solution(mesh):
    in_specs = (
        P(("rep", "seq"), None),
        P(None, ("rep", "seq")),
        P(None, ("rep", "seq")),
        P("rep"),
        P(),
        P(),
        P(None, "seq"),
        P("seq", None),
        P(),
        P(),
    )
    out_specs = P(("rep", "seq"), None)
    body = functools.partial(shards, mesh.shape["seq"], mesh.shape["rep"])
    return jax.shard_map(body, mesh=mesh, in_specs=in_specs, out_specs=out_specs, check_vma=False)
```

time: 199 us -> 56.5 us (0.28)
  blocking collectives: 91.3 us -> 0 us
  Pallas kernels: 0 us -> 54.7 us
  waiting for transfers between devices: 52.9 us -> 0 us
  between operations: 14.3 us -> 0.01 us
  other arithmetic: 13.4 us -> 0 us
  matrix products: 12.9 us -> 0 us
  local copies, waits for them, and re-layouts: 9.39 us -> 1.67 us
  starting transfers between devices: 3.45 us -> 0 us
    all_gather x2 -> x0, blocking collectives: 68 us -> none  [prefix(): lax.all_gather(part.astype(kind), axis)]
    pallas_call x0 -> x1, Pallas kernels: none -> 54.7 us  [shards(): pl.pallas_call(functools.partial(kernel, seq, reps, owners), out_shape=ja...]
    all_gather x2 -> x0, waiting for transfers between devices: 43.3 us -> none  [the longest x1 43.3 us: shards(): lax.all_gather(w_down, 'seq', axis=0, tiled=True)]
    unnamed x1 -> x0, blocking collectives: 23.3 us -> none
    dot_general x11 -> x0, matrix products: 12.9 us -> none  [the longest x2 3.22 us: block_output(): jnp.einsum('hts,hse->hte', weighted, values, preferred_element_type=jnp.f...]
    all_to_all x1 -> x0, waiting for transfers between devices: 8.15 us -> none  [shards(): lax.all_to_all(chosen.reshape(seq_count * per_pair * BR, width), 'seq', s...]
    select_n x21 -> x0, other arithmetic: 4.47 us -> none  [the longest x16 1.73 us: turn(): return jax.tree.map(lambda a, b: jnp.where(reached, a, b), new, before)]
    reduce_sum x5 -> x0, other arithmetic: 3.5 us -> none  [the longest x1 1.39 us: shards(): arriving = jnp.sum(jnp.where(match, all_blocks, 0), axis=0)]
  transfers between devices with their start and end apart: 3 -> 0, of which waited for: 2 -> 0; matrix products, arithmetic and copies ran while one was open for 10% -> 0% of each run, Pallas kernels for 0% -> 0%
where the time goes in v1:
time: 56.5 us; the launch traced here: 56.4 us
  Pallas kernels  54.7 us (97%)
  local copies, waits for them, and re-layouts  1.67 us (3%)
    pallas_call x1, Pallas kernels, shards(): pl.pallas_call(functools.partial(kernel, seq, reps, owners), out_shape=ja...  54.7 us
    unnamed x1, local copies, waits for them, and re-layouts  1.67 us

profile of v1, /device:TPU:0, one launch (start us, length us, event | category | flops | bytes accessed | tf_op | source)
XLA Modules:
  0.0 56.4 jit_solution(16988334252356152750)
XLA Ops:
  0.0 54.7 %shard_map.100 = bf16[256,512]{1,0:T(8,128)(2,1)} custom-call(bf16[128,512]{1,0:T(8,128)(2,1)} %points.1, f32[8,128]{1,0:T(8,128)} %decay_one.1, f32[8,256]{1,0:T(8,128)} %decay_two.1, s32[1,128]{1,0:T(1,128)} %bitcast.1, bf16[512,1536]{1,0:T(8,128)(2,1)} %w_qkv_one.1, bf16[512,512]{1,0:T(8,128)(2,1)} %w_out_one.1, bf16[512,256]{1,0:T(8,128)(2,1)} %w_up.1, ...), custom_call_target="tpu_custom_call" | custom-call | tf_op jit(solution)/shard_map/pallas_call | solution.py:516
  54.7 1.7 %copy.12 = bf16[256,512]{1,0:T(8,128)(2,1)} copy(bf16[256,512]{1,0:T(8,128)(2,1)} %shard_map.100) | data formatting | bytes 524288

commit v2 on v1

--- a/solution.py
+++ b/solution.py
@@ -72,11 +72,23 @@
     return n.bit_length() - 1
 
 
-def project(x, weight, joined):
-    width = x.shape[1]
-    normed = rms(x).astype(BF16)
+def project(normed, weight, joined):
+    width = normed.shape[1]
     joined[:, :width] = (dot(normed, weight[:, :width]) * HEAD_DIM**-0.5).astype(BF16)
     joined[:, width:] = dot(normed, weight[:, width:]).astype(BF16)
+
+
+def sums(decay, width):
+    span = decay.shape[1]
+    later = ones_where(iota((span, span), 0) >= iota((span, span), 1))
+    earlier = ones_where(iota((span, span), 0) <= iota((span, span), 1))
+    heads = ones_where(iota((width, MIXER_STREAMS), 0) // HEAD_DIM == iota((width, MIXER_STREAMS), 1))
+    wide = jnp.zeros((span, width), F32)
+    flat = jnp.zeros((MIXER_STREAMS, span), F32)
+    for piece_of in split3(decay):
+        wide = wide + dot_nt(later, dot(heads, piece_of).astype(BF16))
+        flat = flat + dot(piece_of, earlier)
+    return wide, flat
 
 
 def kernel(
@@ -86,7 +98,7 @@
     wq1, wo1, wq2, wo2, up, down,
     joined_one, joined_two, num_one, num_two, att_one, att_two,
     a_send, a_recv, b_send, b_recv, blk_send, blk_recv, acc,
-    load_sem, own_sem, ring_send, ring_recv, core_send, core_recv,
+    load_sem, own_sem, ring_send, ring_recv, core_send, core_recv, side_send, side_recv, pass_send, pass_recv,
     ex_send, ex_recv,
 ):
     me = lax.axis_index("seq")
@@ -98,6 +110,11 @@
     part = width // halves
     mine = rep % halves
     partner = rep + 1 - 2 * (rep % 2)
+    quarters = 4 if reps % 4 == 0 else halves
+    fine = width // quarters
+    across = rep + 2 - 4 * ((rep // 2) % 2)
+    crossing = quarters == 4
+    neighbours = [partner] * (halves == 2) + [across] * crossing
     groups = width // LANES
     per_group = owners // groups
     state_rows = HEAD_DIM // per_group
@@ -123,9 +140,12 @@
         )
 
     loop(1, seq, greet)
-    if halves == 2:
-        pl.semaphore_signal(barrier, inc=1, device_id={"rep": partner}, device_id_type=MESH)
-    pl.semaphore_wait(barrier, seq - 1 + (1 if halves == 2 else 0))
+    for other in neighbours:
+        pl.semaphore_signal(barrier, inc=1, device_id={"rep": other}, device_id_type=MESH)
+    x = points[...].astype(F32)
+    normed_one = rms(x).astype(BF16)
+    wide, flat = sums(decay_one[...], width)
+    pl.semaphore_wait(barrier, seq - 1 + len(neighbours))
 
     place = jnp.where(me % 2 == 0, me // 2, seq - 1 - me // 2)
 
@@ -135,14 +155,19 @@
 
     neighbour = (at_place(place + 1), at_place(place - 1))
 
+    quarter = (rep % 2) * (quarters // 2) + (rep // 2) % 2 if crossing else mine
+
+    def up_piece(s, index):
+        return up.at[s, pl.ds(pl.multiple_of(index * fine, fine), fine), :]
+
     def piece(w, s):
         if w == 0:
-            return up.at[s, pl.ds(pl.multiple_of(mine * part, part), part), :]
+            return up_piece(s, quarter)
         return down.at[s, :, pl.ds(pl.multiple_of(mine * part, part), part)]
 
     def own_piece(w):
         if w == 0:
-            return w_up.at[pl.ds(pl.multiple_of(mine * part, part), part), :]
+            return w_up.at[pl.ds(pl.multiple_of(quarter * fine, fine), fine), :]
         return w_down.at[:, pl.ds(pl.multiple_of(mine * part, part), part)]
 
     def origin(way, k):
@@ -181,6 +206,39 @@
             device_id_type=MESH,
         )
 
+    def side(way, k):
+        where = up_piece(origin(way, k), quarter)
+        return pltpu.make_async_remote_copy(
+            src_ref=where,
+            dst_ref=where,
+            send_sem=side_send.at[way, k - 1],
+            recv_sem=side_recv.at[way, k - 1],
+            device_id={"rep": across},
+            device_id_type=MESH,
+        )
+
+    def side_arrival(way, k):
+        where = up_piece(origin(way, k), quarter + 1 - 2 * (quarter % 2))
+        return pltpu.make_async_remote_copy(
+            src_ref=where,
+            dst_ref=where,
+            send_sem=side_send.at[way, k - 1],
+            recv_sem=side_recv.at[way, k - 1],
+            device_id={"rep": across},
+            device_id_type=MESH,
+        )
+
+    def hand_on(way, k):
+        where = up_piece(origin(way, k), quarter + 1 - 2 * (quarter % 2))
+        return pltpu.make_async_remote_copy(
+            src_ref=where,
+            dst_ref=where,
+            send_sem=pass_send.at[way, k - 1],
+            recv_sem=pass_recv.at[way, k - 1],
+            device_id={"rep": partner},
+            device_id_type=MESH,
+        )
+
     both = [(way, w) for w in range(2) for way in range(2)]
     last = [(0, 0), (1, 1)]
 
@@ -192,11 +250,24 @@
             ring_arrival(way, w, k).wait_recv()
             if (way, w) in routes_next:
                 ring(way, w, k + 1).start()
+            if crossing and w == 0:
+                side(way, k).start()
             if halves == 2:
                 core(way, w, k).start()
 
-    def relay_step(k):
-        relay(k, routes(k), routes(k + 1) if k < half else [])
+    def relay_part(k, w):
+        relay(
+            k,
+            [route for route in routes(k) if route[1] == w],
+            routes(k + 1) if k < half else [],
+        )
+
+    def crossed(k):
+        if crossing:
+            for way, w in routes(k):
+                if w == 0:
+                    side_arrival(way, k).wait_recv()
+                    hand_on(way, k).start()
 
     for way, w in routes(1):
         ring(way, w, 1, first=True).start()
@@ -266,18 +337,6 @@
             maybe(me < owners, owners == seq, lambda: copy(i, peer).wait_send())
 
         return start, finish, sent
-
-    def sums(decay):
-        span = decay.shape[1]
-        later = ones_where(iota((span, span), 0) >= iota((span, span), 1))
-        earlier = ones_where(iota((span, span), 0) <= iota((span, span), 1))
-        heads = ones_where(iota((width, MIXER_STREAMS), 0) // HEAD_DIM == iota((width, MIXER_STREAMS), 1))
-        wide = jnp.zeros((span, width), F32)
-        flat = jnp.zeros((MIXER_STREAMS, span), F32)
-        for piece_of in split3(decay):
-            wide = wide + dot_nt(later, dot(heads, piece_of).astype(BF16))
-            flat = flat + dot(piece_of, earlier)
-        return wide, flat
 
     def summarise(joined, wide, layer):
         span = joined.shape[0]
@@ -352,23 +411,23 @@
             mean = dot((total * total).astype(BF16), same) * (1.0 / HEAD_DIM)
             att[:, cols] = (total * lax.rsqrt(mean + EPS)).astype(BF16)
 
-    x = points[...].astype(F32)
     loads[0].wait()
-    project(x, wq1, joined_one)
-    wide, flat = sums(decay_one[...])
+    project(normed_one, wq1, joined_one)
     summarise(joined_one, wide, 0)
     start, finish, sent_a1 = to_owners(0, 0)
     loop(1, seq, start)
     own_summary(0)
     many = half > UNROLL // 2
-    pumps = iter(()) if many else iter(range(1, half + 1))
-
-    def pump():
-        k = next(pumps, None)
-        if k is not None:
-            relay_step(k)
-
-    pump()
+    pumps = [] if many else [(k, w) for k in range(1, half + 1) for w in range(2)]
+
+    def pump(count=1):
+        for _ in range(min(count, len(pumps))):
+            k, w = pumps.pop(0)
+            relay_part(k, w)
+            if w == 1:
+                crossed(k)
+
+    pump(2)
     for g in range(groups):
         inner(joined_one, wide, flat, num_one, g)
     loop(1, seq, finish)
@@ -417,7 +476,8 @@
         used = used + dot_nt(jnp.ones((8, chunk), BF16), taken)
     sub = iota((rows_two, all_rows), 0) % BR == iota((rows_two, all_rows), 1) % BR
     gather = jnp.where(sub, placing, 0.0).astype(BF16)
-    wide_two, flat_two = sums(decay_two[...] * used[0:1])
+    wide_two, flat_two = sums(decay_two[...] * used[0:1], width)
+    pump()
 
     loop(1, seq, finish)
     finish_heads(joined_one, wide, num_one, att_one, 0)
@@ -436,6 +496,10 @@
     feed(me)
 
     def take(k):
+        if crossing:
+            for way, w in routes(k):
+                if w == 0:
+                    hand_on(way, k).wait_recv()
         if halves == 2:
             for way, w in routes(k):
                 core(way, w, k).wait_recv()
@@ -447,12 +511,15 @@
         loop(1, half - 1, lambda k: relay(k, both, both))
         relay(half - 1, both, last)
         relay(half, last, [])
+        loop(1, half, crossed)
+        crossed(half)
         loop(1, half, take)
         take(half)
     else:
         for k in range(1, half + 1):
             take(k)
-            pump()
+            pump(1 if k == 1 else 2)
+        assert not pumps
 
     layer_out = acc[...].astype(BF16)
     chosen = dot(scatter, layer_out).astype(BF16)
@@ -465,7 +532,7 @@
     loop(1, seq, lambda i: moved(i).wait_recv())
     placed = dot(gather, blk_recv[...].reshape(all_rows, width))
 
-    project(placed, wq2, joined_two)
+    project(rms(placed).astype(BF16), wq2, joined_two)
     summarise(joined_two, wide_two, 1)
     start, finish, sent_a2 = to_owners(3, 1)
     loop(1, seq, start)
@@ -495,6 +562,9 @@
                 ring(way, w, k).wait_send()
             if halves == 2:
                 core(way, w, k).wait_send()
+            if crossing and w == 0:
+                side(way, k).wait_send()
+                hand_on(way, k).wait_send()
 
     relayed(1)
     loop(2, half, relayed)
@@ -544,6 +614,10 @@
             dma((2, 2, half)),
             dma((2, 2, half)),
             dma((2, 2, half)),
+            dma((2, half)),
+            dma((2, half)),
+            dma((2, half)),
+            dma((2, half)),
             dma((5, seq)),
             dma((5, seq)),
         ],

time: 56.5 us -> 53.5 us (0.947)
  Pallas kernels: 54.7 us -> 51.6 us
    pallas_call x1, Pallas kernels: 54.7 us -> 51.6 us  [shards(): pl.pallas_call(functools.partial(kernel, seq, reps, owners), out_shape=ja...]
where the time goes in v2:
time: 53.5 us; the launch traced here: 53.3 us
  Pallas kernels  51.6 us (96%)
  local copies, waits for them, and re-layouts  1.67 us (3%)
    pallas_call x1, Pallas kernels, shards(): pl.pallas_call(functools.partial(kernel, seq, reps, owners), out_shape=ja...  51.6 us
    unnamed x1, local copies, waits for them, and re-layouts  1.67 us

profile of v2, /device:TPU:0, one launch (start us, length us, event | category | flops | bytes accessed | tf_op | source)
XLA Modules:
  0.0 53.3 jit_solution(8229015196210805221)
XLA Ops:
  0.0 51.6 %shard_map.100 = bf16[256,512]{1,0:T(8,128)(2,1)} custom-call(bf16[128,512]{1,0:T(8,128)(2,1)} %points.1, f32[8,128]{1,0:T(8,128)} %decay_one.1, f32[8,256]{1,0:T(8,128)} %decay_two.1, s32[1,128]{1,0:T(1,128)} %bitcast.1, bf16[512,1536]{1,0:T(8,128)(2,1)} %w_qkv_one.1, bf16[512,512]{1,0:T(8,128)(2,1)} %w_out_one.1, bf16[512,256]{1,0:T(8,128)(2,1)} %w_up.1, ...), custom_call_target="tpu_custom_call" | custom-call | tf_op jit(solution)/shard_map/pallas_call | solution.py:586
  51.6 1.7 %copy.12 = bf16[256,512]{1,0:T(8,128)(2,1)} copy(bf16[256,512]{1,0:T(8,128)(2,1)} %shard_map.100) | data formatting | bytes 524288

commit v3 on v2

--- a/solution.py
+++ b/solution.py
@@ -72,10 +72,14 @@
     return n.bit_length() - 1
 
 
-def project(normed, weight, joined):
+def project_rest(normed, weight, joined):
+    width = normed.shape[1]
+    joined[:, width:] = dot(normed, weight[:, width:]).astype(BF16)
+
+
+def project_queries(normed, weight, joined):
     width = normed.shape[1]
     joined[:, :width] = (dot(normed, weight[:, :width]) * HEAD_DIM**-0.5).astype(BF16)
-    joined[:, width:] = dot(normed, weight[:, width:]).astype(BF16)
 
 
 def sums(decay, width):
@@ -274,11 +278,11 @@
     for copy in loads[1:] + own:
         copy.start()
 
-    def exchange(index, source, target_buf, count):
+    def exchange(index, source, target_buf, place_in=()):
         def copy(i, peer):
             return pltpu.make_async_remote_copy(
-                src_ref=source.at[peer],
-                dst_ref=target_buf.at[me],
+                src_ref=source.at[(peer, *place_in)],
+                dst_ref=target_buf.at[(me, *place_in)],
                 send_sem=ex_send.at[index, i],
                 recv_sem=ex_recv.at[index, i],
                 device_id={"seq": peer},
@@ -288,8 +292,8 @@
         def arrival(i):
             src = lax.rem(me - i + seq, seq)
             return pltpu.make_async_remote_copy(
-                src_ref=target_buf.at[src],
-                dst_ref=target_buf.at[src],
+                src_ref=target_buf.at[(src, *place_in)],
+                dst_ref=target_buf.at[(src, *place_in)],
                 send_sem=ex_send.at[index, i],
                 recv_sem=ex_recv.at[index, i],
                 device_id={"seq": lax.rem(me + i, seq)},
@@ -298,14 +302,22 @@
 
         return copy, arrival
 
+    def far_first(body):
+        middle = seq // 2
+        if seq <= UNROLL:
+            for i in sorted(range(1, seq), key=lambda i: abs(i - middle)):
+                body(i)
+        else:
+            loop(1, seq, body)
+
     def maybe(cond, all_true, body):
         if all_true:
             body()
         else:
             pl.when(cond)(body)
 
-    def to_owners(index, layer):
-        copy, arrival = exchange(index, a_send.at[layer], a_recv.at[layer], owners)
+    def to_owners(index, layer, place_in=()):
+        copy, arrival = exchange(index, a_send.at[layer], a_recv.at[layer], place_in)
 
         def start(i):
             peer = lax.rem(me + i, seq)
@@ -322,7 +334,7 @@
         return start, finish, sent
 
     def from_owners(index, layer):
-        copy, arrival = exchange(index, b_send.at[layer], b_recv.at[layer], seq)
+        copy, arrival = exchange(index, b_send.at[layer], b_recv.at[layer])
 
         def start(i):
             peer = lax.rem(me + i, seq)
@@ -344,18 +356,24 @@
         keys = (joined[:, width : 2 * width].astype(F32) * jnp.exp(total - wide)).astype(BF16)
         values = joined[:, 2 * width :]
         first_head = iota((HEAD_DIM, LANES), 1) < HEAD_DIM
-        tail_row = iota((16, LANES), 0)
         for g in range(groups):
             cols = slice(g * LANES, (g + 1) * LANES)
             state = dot_tn(keys[:, cols], values[:, cols])
             packed = jnp.where(first_head, state[:HEAD_DIM], state[HEAD_DIM:]).astype(BF16)
-            hi, mid, low = (jnp.broadcast_to(t.astype(F32), (16, LANES)) for t in split3(total[:, cols]))
-            tail = jnp.where(tail_row == 0, hi, jnp.where(tail_row == 1, mid, jnp.where(tail_row == 2, low, 0.0)))
-            tail = tail.astype(BF16)
             for r in range(per_group):
                 o = g * per_group + r
                 a_send[layer, o, :state_rows] = packed[r * state_rows : (r + 1) * state_rows]
-                a_send[layer, o, state_rows:] = tail
+
+    def totals(wide, layer):
+        span = wide.shape[0]
+        total = wide[span - 1 : span, :]
+        tail_row = iota((16, LANES), 0)
+        for g in range(groups):
+            cols = slice(g * LANES, (g + 1) * LANES)
+            hi, mid, low = (jnp.broadcast_to(t.astype(F32), (16, LANES)) for t in split3(total[:, cols]))
+            tail = jnp.where(tail_row == 0, hi, jnp.where(tail_row == 1, mid, jnp.where(tail_row == 2, low, 0.0)))
+            for r in range(per_group):
+                a_send[layer, g * per_group + r, state_rows:] = tail.astype(BF16)
 
     def own_summary(layer):
         maybe(me < owners, owners == seq, lambda: store(a_recv, layer, me, a_send[layer, me]))
@@ -399,7 +417,7 @@
             total = total + dot((scores * weight).astype(BF16), value * mask)
         num[:, cols] = total
 
-    def finish_heads(joined, wide, num, att, layer):
+    def finish_heads(joined, grown, num, att, layer):
         same = ones_where(iota((LANES, LANES), 0) // HEAD_DIM == iota((LANES, LANES), 1) // HEAD_DIM)
         for g in range(groups):
             cols = slice(g * LANES, (g + 1) * LANES)
@@ -407,16 +425,18 @@
                 [b_recv[layer, g * per_group + r] for r in range(per_group)], axis=0
             )
             entering = jnp.concatenate([packed, packed], axis=0) * same
-            total = num[:, cols] + dot(joined[:, cols], entering) * jnp.exp(wide[:, cols])
+            total = num[:, cols] + dot(joined[:, cols], entering) * grown[:, cols]
             mean = dot((total * total).astype(BF16), same) * (1.0 / HEAD_DIM)
             att[:, cols] = (total * lax.rsqrt(mean + EPS)).astype(BF16)
 
     loads[0].wait()
-    project(normed_one, wq1, joined_one)
+    project_rest(normed_one, wq1, joined_one)
+    totals(wide, 0)
     summarise(joined_one, wide, 0)
     start, finish, sent_a1 = to_owners(0, 0)
-    loop(1, seq, start)
+    far_first(start)
     own_summary(0)
+    project_queries(normed_one, wq1, joined_one)
     many = half > UNROLL // 2
     pumps = [] if many else [(k, w) for k in range(1, half + 1) for w in range(2)]
 
@@ -433,7 +453,7 @@
     loop(1, seq, finish)
     prefix(0)
     start, finish, sent_b1 = from_owners(1, 0)
-    loop(1, seq, start)
+    far_first(start)
     pump()
 
     blocks = target.shape[1]
@@ -477,10 +497,14 @@
     sub = iota((rows_two, all_rows), 0) % BR == iota((rows_two, all_rows), 1) % BR
     gather = jnp.where(sub, placing, 0.0).astype(BF16)
     wide_two, flat_two = sums(decay_two[...] * used[0:1], width)
+    totals(wide_two, 1)
+    start_tail, finish_tail, sent_tail = to_owners(5, 1, (pl.ds(state_rows, 16),))
+    loop(1, seq, start_tail)
     pump()
 
+    grown = jnp.exp(wide)
     loop(1, seq, finish)
-    finish_heads(joined_one, wide, num_one, att_one, 0)
+    finish_heads(joined_one, grown, num_one, att_one, 0)
     loads[1].wait()
     first = (x + dot(att_one[...], wo1[...])).astype(BF16)
     normed = rms(first.astype(F32)).astype(BF16)
@@ -525,32 +549,33 @@
     chosen = dot(scatter, layer_out).astype(BF16)
     for j in range(seq):
         blk_send[j] = chosen[j * pair_rows : (j + 1) * pair_rows]
-    move, moved = exchange(2, blk_send, blk_recv, seq)
-    loop(1, seq, lambda i: move(i, lax.rem(me + i, seq)).start())
+    move, moved = exchange(2, blk_send, blk_recv)
+    far_first(lambda i: move(i, lax.rem(me + i, seq)).start())
     blk_recv[me] = blk_send[me]
     loads[2].wait()
+    loop(1, seq, finish_tail)
     loop(1, seq, lambda i: moved(i).wait_recv())
     placed = dot(gather, blk_recv[...].reshape(all_rows, width))
 
-    project(rms(placed).astype(BF16), wq2, joined_two)
+    normed_two = rms(placed).astype(BF16)
+    project_rest(normed_two, wq2, joined_two)
     summarise(joined_two, wide_two, 1)
-    start, finish, sent_a2 = to_owners(3, 1)
-    loop(1, seq, start)
+    start, finish, sent_a2 = to_owners(3, 1, (pl.ds(0, state_rows),))
+    far_first(start)
     own_summary(1)
+    project_queries(normed_two, wq2, joined_two)
     for g in range(groups // 2):
         inner(joined_two, wide_two, flat_two, num_two, g)
     loop(1, seq, finish)
     prefix(1)
     start, finish, sent_b2 = from_owners(4, 1)
-    loop(1, seq, start)
+    far_first(start)
     for g in range(groups // 2, groups):
         inner(joined_two, wide_two, flat_two, num_two, g)
     loads[3].wait()
-    loop(1, seq, finish)
-    finish_heads(joined_two, wide_two, num_two, att_two, 1)
-    out[...] = (placed + dot(att_two[...], wo2[...])).astype(BF16)
-
-    for sent in (sent_a1, sent_b1, sent_a2, sent_b2):
+    grown_two = jnp.exp(wide_two)
+
+    for sent in (sent_a1, sent_b1, sent_tail, sent_a2):
         loop(1, seq, sent)
     loop(1, seq, lambda i: move(i, lax.rem(me + i, seq)).wait_send())
     for way, w in routes(1):
@@ -569,6 +594,10 @@
     relayed(1)
     loop(2, half, relayed)
     relayed(half)
+    loop(1, seq, finish)
+    finish_heads(joined_two, grown_two, num_two, att_two, 1)
+    out[...] = (placed + dot(att_two[...], wo2[...])).astype(BF16)
+    loop(1, seq, sent_b2)
 
 
 def shards(seq, reps, points, decay_one, decay_two, block_target, w_qkv_one, w_out_one, w_up, w_down, w_qkv_two, w_out_two):
@@ -618,8 +647,8 @@
             dma((2, half)),
             dma((2, half)),
             dma((2, half)),
-            dma((5, seq)),
-            dma((5, seq)),
+            dma((6, seq)),
+            dma((6, seq)),
         ],
         compiler_params=pltpu.CompilerParams(
             collective_id=0, has_side_effects=True, vmem_limit_bytes=56 * 1024 * 1024

time: 53.5 us -> 54.4 us (1.017)
  Pallas kernels: 51.6 us -> 52.6 us
    pallas_call x1, Pallas kernels: 51.6 us -> 52.6 us  [shards(): pl.pallas_call(functools.partial(kernel, seq, reps, owners), out_shape=ja...]
where the time goes in v3:
time: 54.4 us; the launch traced here: 54.2 us
  Pallas kernels  52.6 us (97%)
  local copies, waits for them, and re-layouts  1.67 us (3%)
    pallas_call x1, Pallas kernels, shards(): pl.pallas_call(functools.partial(kernel, seq, reps, owners), out_shape=ja...  52.6 us
    unnamed x1, local copies, waits for them, and re-layouts  1.67 us

profile of v3, /device:TPU:0, one launch (start us, length us, event | category | flops | bytes accessed | tf_op | source)
XLA Modules:
  0.0 54.2 jit_solution(9857645009856078978)
XLA Ops:
  0.0 52.6 %shard_map.100 = bf16[256,512]{1,0:T(8,128)(2,1)} custom-call(bf16[128,512]{1,0:T(8,128)(2,1)} %points.1, f32[8,128]{1,0:T(8,128)} %decay_one.1, f32[8,256]{1,0:T(8,128)} %decay_two.1, s32[1,128]{1,0:T(1,128)} %bitcast.1, bf16[512,1536]{1,0:T(8,128)(2,1)} %w_qkv_one.1, bf16[512,512]{1,0:T(8,128)(2,1)} %w_out_one.1, bf16[512,256]{1,0:T(8,128)(2,1)} %w_up.1, ...), custom_call_target="tpu_custom_call" | custom-call | tf_op jit(solution)/shard_map/pallas_call | solution.py:615
  52.6 1.7 %copy.12 = bf16[256,512]{1,0:T(8,128)(2,1)} copy(bf16[256,512]{1,0:T(8,128)(2,1)} %shard_map.100) | data formatting | bytes 524288

commit v4 on v3

--- a/solution.py
+++ b/solution.py
@@ -72,14 +72,30 @@
     return n.bit_length() - 1
 
 
+def strips(start, stop, size, body):
+    def step(n, carry):
+        body(pl.ds(pl.multiple_of(n * size, size), size))
+        return carry
+
+    lax.fori_loop(start // size, stop // size, step, 0)
+
+
 def project_rest(normed, weight, joined):
     width = normed.shape[1]
-    joined[:, width:] = dot(normed, weight[:, width:]).astype(BF16)
+
+    def strip(cols):
+        joined[:, cols] = dot(normed, weight[:, cols]).astype(BF16)
+
+    strips(width, 3 * width, 2 * LANES, strip)
 
 
 def project_queries(normed, weight, joined):
     width = normed.shape[1]
-    joined[:, :width] = (dot(normed, weight[:, :width]) * HEAD_DIM**-0.5).astype(BF16)
+
+    def strip(cols):
+        joined[:, cols] = (dot(normed, weight[:, cols]) * HEAD_DIM**-0.5).astype(BF16)
+
+    strips(0, width, 2 * LANES, strip)
 
 
 def sums(decay, width):
@@ -101,7 +117,7 @@
     out,
     wq1, wo1, wq2, wo2, up, down,
     joined_one, joined_two, num_one, num_two, att_one, att_two,
-    a_send, a_recv, b_send, b_recv, blk_send, blk_recv, acc,
+    wide_one, wide_two, flat_one, flat_two, normed, held, a_send, a_recv, b_send, b_recv, blk_send, blk_recv, acc,
     load_sem, own_sem, ring_send, ring_recv, core_send, core_recv, side_send, side_recv, pass_send, pass_recv,
     ex_send, ex_recv,
 ):
@@ -148,7 +164,7 @@
         pl.semaphore_signal(barrier, inc=1, device_id={"rep": other}, device_id_type=MESH)
     x = points[...].astype(F32)
     normed_one = rms(x).astype(BF16)
-    wide, flat = sums(decay_one[...], width)
+    wide_one[...], flat_one[...] = sums(decay_one[...], width)
     pl.semaphore_wait(barrier, seq - 1 + len(neighbours))
 
     place = jnp.where(me % 2 == 0, me // 2, seq - 1 - me // 2)
@@ -175,7 +191,7 @@
         return w_down.at[:, pl.ds(pl.multiple_of(mine * part, part), part)]
 
     def origin(way, k):
-        return at_place(place - k if way == 0 else place + k)
+        return at_place(place + (2 * way - 1) * k)
 
     def ring(way, w, k, first=False):
         where = piece(w, me if first else origin(way, k - 1))
@@ -350,19 +366,27 @@
 
         return start, finish, sent
 
+    def each_group(body, first=0, stop=groups):
+        def step(g, carry):
+            body(g, lambda start: pl.ds(pl.multiple_of(start + g * LANES, LANES), LANES))
+            return carry
+
+        lax.fori_loop(first, stop, step, 0)
+
     def summarise(joined, wide, layer):
         span = joined.shape[0]
-        total = wide[span - 1 : span, :]
-        keys = (joined[:, width : 2 * width].astype(F32) * jnp.exp(total - wide)).astype(BF16)
-        values = joined[:, 2 * width :]
         first_head = iota((HEAD_DIM, LANES), 1) < HEAD_DIM
-        for g in range(groups):
-            cols = slice(g * LANES, (g + 1) * LANES)
-            state = dot_tn(keys[:, cols], values[:, cols])
+
+        def group(g, cols):
+            sums_here = wide[:, cols(0)]
+            decay = jnp.exp(sums_here[span - 1 : span, :] - sums_here)
+            keys = (joined[:, cols(width)].astype(F32) * decay).astype(BF16)
+            state = dot_tn(keys, joined[:, cols(2 * width)])
             packed = jnp.where(first_head, state[:HEAD_DIM], state[HEAD_DIM:]).astype(BF16)
             for r in range(per_group):
-                o = g * per_group + r
-                a_send[layer, o, :state_rows] = packed[r * state_rows : (r + 1) * state_rows]
+                a_send[layer, g * per_group + r, :state_rows] = packed[r * state_rows : (r + 1) * state_rows]
+
+        each_group(group)
 
     def totals(wide, layer):
         span = wide.shape[0]
@@ -400,39 +424,44 @@
 
         maybe(me < owners, owners == seq, run)
 
-    def inner(joined, wide, flat, num, g):
+    def inner(joined, wide, flat, num, first=0, stop=groups):
         span = joined.shape[0]
-        cols = slice(g * LANES, (g + 1) * LANES)
-        query = joined[:, cols]
-        key = joined[:, width + g * LANES : width + (g + 1) * LANES]
-        value = joined[:, 2 * width + g * LANES : 2 * width + (g + 1) * LANES]
-        causal = iota((span, span), 0) >= iota((span, span), 1)
-        total = jnp.zeros((span, LANES), F32)
-        for a in range(2):
-            mask = ones_where(iota((1, LANES), 1) // HEAD_DIM == a)
-            h = 2 * g + a
-            gap = wide[:, h * HEAD_DIM : h * HEAD_DIM + 1] - flat[h : h + 1, :]
-            weight = jnp.exp(jnp.where(causal, gap, -1e30))
-            scores = dot_nt(query, key * mask)
-            total = total + dot((scores * weight).astype(BF16), value * mask)
-        num[:, cols] = total
-
-    def finish_heads(joined, grown, num, att, layer):
+
+        def group(g, cols):
+            query = joined[:, cols(0)]
+            key = joined[:, cols(width)]
+            value = joined[:, cols(2 * width)]
+            sums_here = wide[:, cols(0)]
+            causal = iota((span, span), 0) >= iota((span, span), 1)
+            total = jnp.zeros((span, LANES), F32)
+            for a in range(2):
+                mask = ones_where(iota((1, LANES), 1) // HEAD_DIM == a)
+                gap = sums_here[:, a * HEAD_DIM : a * HEAD_DIM + 1] - flat[pl.ds(2 * g + a, 1), :]
+                weight = jnp.exp(jnp.where(causal, gap, -1e30))
+                scores = dot_nt(query, key * mask)
+                total = total + dot((scores * weight).astype(BF16), value * mask)
+            num[:, cols(0)] = total
+
+        each_group(group, first, stop)
+
+    def finish_heads(joined, wide, num, att, layer):
         same = ones_where(iota((LANES, LANES), 0) // HEAD_DIM == iota((LANES, LANES), 1) // HEAD_DIM)
-        for g in range(groups):
-            cols = slice(g * LANES, (g + 1) * LANES)
+
+        def group(g, cols):
             packed = jnp.concatenate(
                 [b_recv[layer, g * per_group + r] for r in range(per_group)], axis=0
             )
             entering = jnp.concatenate([packed, packed], axis=0) * same
-            total = num[:, cols] + dot(joined[:, cols], entering) * grown[:, cols]
+            total = num[:, cols(0)] + dot(joined[:, cols(0)], entering) * jnp.exp(wide[:, cols(0)])
             mean = dot((total * total).astype(BF16), same) * (1.0 / HEAD_DIM)
-            att[:, cols] = (total * lax.rsqrt(mean + EPS)).astype(BF16)
+            att[:, cols(0)] = (total * lax.rsqrt(mean + EPS)).astype(BF16)
+
+        each_group(group)
 
     loads[0].wait()
     project_rest(normed_one, wq1, joined_one)
-    totals(wide, 0)
-    summarise(joined_one, wide, 0)
+    totals(wide_one, 0)
+    summarise(joined_one, wide_one, 0)
     start, finish, sent_a1 = to_owners(0, 0)
     far_first(start)
     own_summary(0)
@@ -448,8 +477,7 @@
                 crossed(k)
 
     pump(2)
-    for g in range(groups):
-        inner(joined_one, wide, flat, num_one, g)
+    inner(joined_one, wide_one, flat_one, num_one)
     loop(1, seq, finish)
     prefix(0)
     start, finish, sent_b1 = from_owners(1, 0)
@@ -496,54 +524,60 @@
         used = used + dot_nt(jnp.ones((8, chunk), BF16), taken)
     sub = iota((rows_two, all_rows), 0) % BR == iota((rows_two, all_rows), 1) % BR
     gather = jnp.where(sub, placing, 0.0).astype(BF16)
-    wide_two, flat_two = sums(decay_two[...] * used[0:1], width)
+    wide_two[...], flat_two[...] = sums(decay_two[...] * used[0:1], width)
     totals(wide_two, 1)
     start_tail, finish_tail, sent_tail = to_owners(5, 1, (pl.ds(state_rows, 16),))
     loop(1, seq, start_tail)
     pump()
 
-    grown = jnp.exp(wide)
     loop(1, seq, finish)
-    finish_heads(joined_one, grown, num_one, att_one, 0)
+    finish_heads(joined_one, wide_one, num_one, att_one, 0)
     loads[1].wait()
     first = (x + dot(att_one[...], wo1[...])).astype(BF16)
-    normed = rms(first.astype(F32)).astype(BF16)
+    normed[...] = rms(first.astype(F32)).astype(BF16)
 
     def feed(s):
-        hidden = gelu(dot(normed, up[s])).astype(BF16)
+        hidden = gelu(dot(normed[...], up[s])).astype(BF16)
         acc[...] += dot(hidden, down[s])
 
     acc[...] = first.astype(F32)
     pump()
     for copy in own:
         copy.wait()
-    feed(me)
-
-    def take(k):
-        if crossing:
-            for way, w in routes(k):
-                if w == 0:
-                    hand_on(way, k).wait_recv()
-        if halves == 2:
-            for way, w in routes(k):
-                core(way, w, k).wait_recv()
-        feed(origin(0, k))
-        if not (isinstance(k, int) and k == half):
-            feed(origin(1, k))
-
     if many:
         loop(1, half - 1, lambda k: relay(k, both, both))
         relay(half - 1, both, last)
         relay(half, last, [])
         loop(1, half, crossed)
         crossed(half)
-        loop(1, half, take)
-        take(half)
-    else:
-        for k in range(1, half + 1):
-            take(k)
-            pump(1 if k == 1 else 2)
-        assert not pumps
+
+    def take(j, carry):
+        k, way = (j + 1) // 2, lax.rem(j + 1, 2)
+
+        @pl.when(jnp.logical_and(j > 0, j < seq - 1))
+        def _():
+            if halves == 2:
+                core(way, 0, k).wait_recv()
+                core(way, 1, k).wait_recv()
+            if crossing:
+                hand_on(way, k).wait_recv()
+
+        @pl.when(j == seq - 1)
+        def _():
+            if halves == 2:
+                core(0, 0, half).wait_recv()
+                core(1, 1, half).wait_recv()
+            if crossing:
+                hand_on(0, half).wait_recv()
+
+        feed(at_place(place + (2 * way - 1) * k))
+        if not many:
+            for count, after in ((1, seq // 4), (2, seq // 2)):
+                pl.when(j == after)(functools.partial(pump, count))
+        return carry
+
+    lax.fori_loop(0, seq, take, 0)
+    assert not pumps
 
     layer_out = acc[...].astype(BF16)
     chosen = dot(scatter, layer_out).astype(BF16)
@@ -556,6 +590,7 @@
     loop(1, seq, finish_tail)
     loop(1, seq, lambda i: moved(i).wait_recv())
     placed = dot(gather, blk_recv[...].reshape(all_rows, width))
+    held[...] = placed
 
     normed_two = rms(placed).astype(BF16)
     project_rest(normed_two, wq2, joined_two)
@@ -564,16 +599,13 @@
     far_first(start)
     own_summary(1)
     project_queries(normed_two, wq2, joined_two)
-    for g in range(groups // 2):
-        inner(joined_two, wide_two, flat_two, num_two, g)
+    inner(joined_two, wide_two, flat_two, num_two, 0, groups // 2)
     loop(1, seq, finish)
     prefix(1)
     start, finish, sent_b2 = from_owners(4, 1)
     far_first(start)
-    for g in range(groups // 2, groups):
-        inner(joined_two, wide_two, flat_two, num_two, g)
+    inner(joined_two, wide_two, flat_two, num_two, groups // 2, groups)
     loads[3].wait()
-    grown_two = jnp.exp(wide_two)
 
     for sent in (sent_a1, sent_b1, sent_tail, sent_a2):
         loop(1, seq, sent)
@@ -595,8 +627,12 @@
     loop(2, half, relayed)
     relayed(half)
     loop(1, seq, finish)
-    finish_heads(joined_two, grown_two, num_two, att_two, 1)
-    out[...] = (placed + dot(att_two[...], wo2[...])).astype(BF16)
+    finish_heads(joined_two, wide_two, num_two, att_two, 1)
+
+    def strip(cols):
+        out[:, cols] = (held[:, cols] + dot(att_two[...], wo2[:, cols])).astype(BF16)
+
+    strips(0, width, 2 * LANES, strip)
     loop(1, seq, sent_b2)
 
 
@@ -630,6 +666,12 @@
             pltpu.VMEM((rows_two, width), F32),
             pltpu.VMEM((rows, width), BF16),
             pltpu.VMEM((rows_two, width), BF16),
+            pltpu.VMEM((rows, width), F32),
+            pltpu.VMEM((rows_two, width), F32),
+            pltpu.VMEM((MIXER_STREAMS, rows), F32),
+            pltpu.VMEM((MIXER_STREAMS, rows_two), F32),
+            pltpu.VMEM((rows, width), BF16),
+            pltpu.VMEM((rows_two, width), F32),
             pltpu.VMEM((2, owners, state_rows + 16, LANES), BF16),
             pltpu.VMEM((2, seq, state_rows + 16, LANES), BF16),
             pltpu.VMEM((2, seq, state_rows, LANES), BF16),

time: 54.4 us -> 58.1 us (1.068)
  Pallas kernels: 52.6 us -> 56.3 us
    pallas_call x1, Pallas kernels: 52.6 us -> 56.3 us  [shards(): pl.pallas_call(functools.partial(kernel, seq, reps, owners), out_shape=ja...]
where the time goes in v4:
time: 58.1 us; the launch traced here: 58 us
  Pallas kernels  56.3 us (97%)
  local copies, waits for them, and re-layouts  1.67 us (3%)
    pallas_call x1, Pallas kernels, shards(): pl.pallas_call(functools.partial(kernel, seq, reps, owners), out_shape=ja...  56.3 us
    unnamed x1, local copies, waits for them, and re-layouts  1.67 us

profile of v4, /device:TPU:0, one launch (start us, length us, event | category | flops | bytes accessed | tf_op | source)
XLA Modules:
  0.0 58.0 jit_solution(12042330552570059452)
XLA Ops:
  0.0 56.3 %shard_map.100 = bf16[256,512]{1,0:T(8,128)(2,1)} custom-call(bf16[128,512]{1,0:T(8,128)(2,1)} %points.1, f32[8,128]{1,0:T(8,128)} %decay_one.1, f32[8,256]{1,0:T(8,128)} %decay_two.1, s32[1,128]{1,0:T(1,128)} %bitcast.1, bf16[512,1536]{1,0:T(8,128)(2,1)} %w_qkv_one.1, bf16[512,512]{1,0:T(8,128)(2,1)} %w_out_one.1, bf16[512,256]{1,0:T(8,128)(2,1)} %w_up.1, ...), custom_call_target="tpu_custom_call" | custom-call | tf_op jit(solution)/shard_map/pallas_call | solution.py:651
  56.3 1.7 %copy.12 = bf16[256,512]{1,0:T(8,128)(2,1)} copy(bf16[256,512]{1,0:T(8,128)(2,1)} %shard_map.100) | data formatting | bytes 524288

commit v5 on v3

--- a/solution.py
+++ b/solution.py
@@ -97,8 +97,10 @@
 
 def kernel(
     seq, reps, owners,
-    points, decay_one, decay_two, target, w_qkv_one, w_out_one, w_up, w_down, w_qkv_two, w_out_two,
+    points_in, decay_one_in, decay_two_in, target_in,
+    w_qkv_one, w_out_one, w_up, w_down, w_qkv_two, w_out_two,
     out,
+    points, decay_one, decay_two, target,
     wq1, wo1, wq2, wo2, up, down,
     joined_one, joined_two, num_one, num_two, att_one, att_two,
     a_send, a_recv, b_send, b_recv, blk_send, blk_recv, acc,
@@ -130,7 +132,12 @@
             ((w_qkv_one, wq1), (w_out_one, wo1), (w_qkv_two, wq2), (w_out_two, wo2))
         )
     ]
-    loads[0].start()
+    small = [
+        pltpu.make_async_copy(src, dst, load_sem.at[4 + i])
+        for i, (src, dst) in enumerate(
+            ((points_in, points), (decay_one_in, decay_one), (decay_two_in, decay_two), (target_in, target))
+        )
+    ]
     own = [
         pltpu.make_async_copy(w_up, up.at[me], own_sem.at[0]),
         pltpu.make_async_copy(w_down, down.at[me], own_sem.at[1]),
@@ -146,6 +153,11 @@
     loop(1, seq, greet)
     for other in neighbours:
         pl.semaphore_signal(barrier, inc=1, device_id={"rep": other}, device_id_type=MESH)
+    for copy in small:
+        copy.start()
+    loads[0].start()
+    for copy in small:
+        copy.wait()
     x = points[...].astype(F32)
     normed_one = rms(x).astype(BF16)
     wide, flat = sums(decay_one[...], width)
@@ -507,14 +519,23 @@
     finish_heads(joined_one, grown, num_one, att_one, 0)
     loads[1].wait()
     first = (x + dot(att_one[...], wo1[...])).astype(BF16)
-    normed = rms(first.astype(F32)).astype(BF16)
+
+    chosen = dot(scatter, first).astype(BF16)
+    for j in range(seq):
+        blk_send[j] = chosen[j * pair_rows : (j + 1) * pair_rows]
+    move, moved = exchange(2, blk_send, blk_recv)
+    far_first(lambda i: move(i, lax.rem(me + i, seq)).start())
+    blk_recv[me] = blk_send[me]
+    pump(3)
+    loop(1, seq, lambda i: moved(i).wait_recv())
+    arrived = dot(gather, blk_recv[...].reshape(all_rows, width))
+    normed = rms(arrived).astype(BF16)
 
     def feed(s):
         hidden = gelu(dot(normed, up[s])).astype(BF16)
         acc[...] += dot(hidden, down[s])
 
-    acc[...] = first.astype(F32)
-    pump()
+    acc[...] = arrived
     for copy in own:
         copy.wait()
     feed(me)
@@ -542,20 +563,12 @@
     else:
         for k in range(1, half + 1):
             take(k)
-            pump(1 if k == 1 else 2)
+            pump(2)
         assert not pumps
 
-    layer_out = acc[...].astype(BF16)
-    chosen = dot(scatter, layer_out).astype(BF16)
-    for j in range(seq):
-        blk_send[j] = chosen[j * pair_rows : (j + 1) * pair_rows]
-    move, moved = exchange(2, blk_send, blk_recv)
-    far_first(lambda i: move(i, lax.rem(me + i, seq)).start())
-    blk_recv[me] = blk_send[me]
     loads[2].wait()
     loop(1, seq, finish_tail)
-    loop(1, seq, lambda i: moved(i).wait_recv())
-    placed = dot(gather, blk_recv[...].reshape(all_rows, width))
+    placed = acc[...].astype(BF16).astype(F32)
 
     normed_two = rms(placed).astype(BF16)
     project_rest(normed_two, wq2, joined_two)
@@ -615,9 +628,13 @@
     return pl.pallas_call(
         functools.partial(kernel, seq, reps, owners),
         out_shape=jax.ShapeDtypeStruct((rows_two, width), BF16),
-        in_specs=[vmem] * 4 + [anywhere] * 6,
+        in_specs=[anywhere] * 10,
         out_specs=vmem,
         scratch_shapes=[
+            pltpu.VMEM(points.shape, BF16),
+            pltpu.VMEM(decay_one.shape, F32),
+            pltpu.VMEM(decay_two.shape, F32),
+            pltpu.VMEM((1, block_target.size), jnp.int32),
             pltpu.VMEM(w_qkv_one.shape, BF16),
             pltpu.VMEM(w_out_one.shape, BF16),
             pltpu.VMEM(w_qkv_two.shape, BF16),
@@ -636,8 +653,8 @@
             pltpu.VMEM((2, owners, state_rows, LANES), BF16),
             pltpu.VMEM((seq, pair_rows, width), BF16),
             pltpu.VMEM((seq, pair_rows, width), BF16),
-            pltpu.VMEM((rows, width), F32),
-            dma((4,)),
+            pltpu.VMEM((rows_two, width), F32),
+            dma((8,)),
             dma((2,)),
             dma((2, 2, half)),
             dma((2, 2, half)),

time: 54.4 us -> 49.6 us (0.912)
  Pallas kernels: 52.6 us -> 47.8 us
    pallas_call x1, Pallas kernels: 52.6 us -> 47.8 us  [shards(): pl.pallas_call(functools.partial(kernel, seq, reps, owners), out_shape=ja...]
where the time goes in v5:
time: 49.6 us; the launch traced here: 49.4 us
  Pallas kernels  47.8 us (96%)
  local copies, waits for them, and re-layouts  1.67 us (3%)
    pallas_call x1, Pallas kernels, shards(): pl.pallas_call(functools.partial(kernel, seq, reps, owners), out_shape=ja...  47.8 us
    unnamed x1, local copies, waits for them, and re-layouts  1.67 us

profile of v5, /device:TPU:0, one launch (start us, length us, event | category | flops | bytes accessed | tf_op | source)
XLA Modules:
  0.0 49.4 jit_solution(13744608399949066174)
XLA Ops:
  0.0 47.8 %shard_map.100 = bf16[256,512]{1,0:T(8,128)(2,1)} custom-call(bf16[128,512]{1,0:T(8,128)(2,1)} %points_in.1, f32[8,128]{1,0:T(8,128)} %decay_one_in.1, f32[8,256]{1,0:T(8,128)} %decay_two_in.1, s32[1,128]{1,0:T(1,128)} %bitcast.1, bf16[512,1536]{1,0:T(8,128)(2,1)} %w_qkv_one.1, bf16[512,512]{1,0:T(8,128)(2,1)} %w_out_one.1, bf16[512,256]{1,0:T(8,128)(2,1)} %w_up.1, ...), custom_call_target="tpu_custom_call" | custom-call | tf_op jit(solution)/shard_map/pallas_call | solution.py:628
  47.8 1.7 %copy.12 = bf16[256,512]{1,0:T(8,128)(2,1)} copy(bf16[256,512]{1,0:T(8,128)(2,1)} %shard_map.100) | data formatting | bytes 524288
